TPU v7x, 256 devices: a whole 4x4x8 slice. The times are simulated.
256 devices in a mesh: seq: 32 (over x, z_lo, core), tp: 8 (over y, z_hi).
Axes of the slice: x: 4, y: 4, z: 8 (z_hi: 2, z_lo: 4; z = z_hi * 4 + z_lo), core: 2. Of those that a mesh axis runs over, the one named last changes fastest.
Arguments:
- inner_gate: bfloat16 [8192, 8192], P('seq', 'tp'), may hold values from -6 to 6
- values: bfloat16 [8192, 8192], P('seq', 'tp'), may hold values from -6 to 6
- outer_gate: bfloat16 [8192, 8192], P('seq', 'tp'), may hold values from -6 to 6
- filters: float32 [8192, 8192], P('seq', 'tp'), may hold values from -0.0625 to 0.0625
- skip_gain: float32 [8192], P('tp'), may hold values from 0.5 to 2
- w_out: bfloat16 [8192, 4096], P('tp'), may hold values from -0.09375 to 0.09375
Outputs:
- mixed_out: bfloat16 [8192, 4096], P('seq', 'tp')
All inputs are finite; a program needn't handle non-finite values.
Results may differ from a plain program's by a relative error of at most 0.015.
Values may be sent and summed in bfloat16 or wider, within the bound.
A program may use at most 192 MiB of HBM per device.

v0:
```python
import math

import jax
import jax.numpy as jnp
from jax import lax
from jax.sharding import PartitionSpec as P

HIGH = lax.Precision.HIGHEST


def angle_table(first, second, modulus):
    product_idx = jnp.mod(first[:, None] * second[None, :], modulus)
    angles = product_idx.astype(jnp.float32) * (2.0 * math.pi / modulus)
    return (jnp.cos(angles), jnp.sin(angles))


def local(inner_gate, values, outer_gate, filters, skip_gain, w_out):
    seq_count = lax.axis_size("seq")
    rows_dev = inner_gate.shape[0]
    part_len = rows_dev // seq_count
    total_len = 2 * seq_count * rows_dev
    position = lax.axis_index("seq")
    product = inner_gate.astype(jnp.float32) * values.astype(jnp.float32)
    paired = jnp.stack([product, filters])[:, None]
    block = lax.all_to_all(paired, "seq", split_axis=2, concat_axis=1, tiled=True)
    freq_idx = jnp.arange(2 * seq_count, dtype=jnp.int32)
    cos_tab, sin_tab = angle_table(freq_idx, jnp.arange(seq_count, dtype=jnp.int32), 2 * seq_count)
    real_part = jnp.einsum("ks,gstc->gktc", cos_tab, block, precision=HIGH)
    imag_part = -jnp.einsum("ks,gstc->gktc", sin_tab, block, precision=HIGH)
    offsets = position * part_len + jnp.arange(part_len, dtype=jnp.int32)
    cos_tw, sin_tw = angle_table(freq_idx, offsets, total_len)
    cos_tw = cos_tw[None, :, :, None]
    sin_tw = sin_tw[None, :, :, None]
    out_real = real_part * cos_tw + imag_part * sin_tw
    out_imag = imag_part * cos_tw - real_part * sin_tw
    spread = jnp.stack([out_real, out_imag], axis=1)
    block = lax.all_to_all(spread, "seq", split_axis=2, concat_axis=3, tiled=True)
    full_idx = jnp.arange(rows_dev, dtype=jnp.int32)
    cos_full, sin_full = angle_table(full_idx, full_idx, rows_dev)

    def apply(table, operand):
        return jnp.einsum("kt,jtc->jkc", table, operand, precision=HIGH)

    def forward(real_in, imag_in):
        return (
            apply(cos_full, real_in) + apply(sin_full, imag_in),
            apply(cos_full, imag_in) - apply(sin_full, real_in),
        )

    z_real, z_imag = forward(block[0, 0], block[0, 1])
    h_real, h_imag = forward(block[1, 0], block[1, 1])
    y_real = z_real * h_real - z_imag * h_imag
    y_imag = z_real * h_imag + z_imag * h_real
    g_real = apply(cos_full, y_real) - apply(sin_full, y_imag)
    g_imag = apply(cos_full, y_imag) + apply(sin_full, y_real)
    coarse = 2 * position + jnp.arange(2, dtype=jnp.int32)
    cos_tw, sin_tw = angle_table(coarse, full_idx, total_len)
    cos_tw = cos_tw[:, :, None]
    sin_tw = sin_tw[:, :, None]
    out_real = g_real * cos_tw - g_imag * sin_tw
    out_imag = g_real * sin_tw + g_imag * cos_tw
    spectra = jnp.stack([out_real, out_imag])
    block = lax.all_to_all(spectra, "seq", split_axis=2, concat_axis=1, tiled=True)
    cos_tab, sin_tab = angle_table(
        jnp.arange(seq_count, dtype=jnp.int32),
        jnp.arange(2 * seq_count, dtype=jnp.int32),
        2 * seq_count,
    )
    summed = jnp.einsum("sk,ktc->stc", cos_tab, block[0], precision=HIGH) - jnp.einsum(
        "sk,ktc->stc", sin_tab, block[1], precision=HIGH
    )
    moved = summed / total_len
    conv = lax.all_to_all(moved, "seq", split_axis=0, concat_axis=1, tiled=True)[0]
    mixed = (outer_gate.astype(jnp.float32) * (conv + skip_gain[None, :] * product)).astype(
        jnp.bfloat16
    )
    summed = lax.psum_scatter(
        lax.dot_general(
            w_out, mixed, (((0,), (1,)), ((), ())), preferred_element_type=jnp.float32
        ).astype(jnp.bfloat16),
        "tp",
        scatter_dimension=0,
        tiled=True,
    ).astype(jnp.float32)
    return summed.T.astype(jnp.bfloat16)


def solution(mesh):
    in_specs = (
        P("seq", "tp"),
        P("seq", "tp"),
        P("seq", "tp"),
        P("seq", "tp"),
        P("tp"),
        P("tp", None),
    )
    out_specs = P("seq", "tp")
    return jax.shard_map(local, mesh=mesh, in_specs=in_specs, out_specs=out_specs, check_vma=False)
```

profile of v0, /device:TPU:1, one launch (start us, length us, event | category | flops | bytes accessed | tf_op | source)
XLA Modules:
  0.0 618.2 jit_solution(17306423147479092628)
XLA Ops:
  6.5 1.5 fusion.38
  8.0 0.1 copy-done.1
  8.1 0.2 maximum_bitcast_fusion
  8.3 3.0 copy.35
  11.3 10.4 %all-to-all-start = ((f32[2,1,256,1024]{3,0,1,2:T(2,128)}), f32[2,1,256,1024]{3,0,1,2:T(2,128)S(1)}, u32[]{:S(2)}, u32[]{:S(2)}) async-start(f32[2,1,256,1024]{3,0,1,2:T(2,128)} %copy.35), calls=%async_computation | async-start | bytes 4194304 | tf_op jit(solution)/shard_map/all_to_all | solution.py:25
  21.7 0.1 fusion.108
  21.8 49.2 %all-to-all-done = f32[2,1,256,1024]{3,0,1,2:T(2,128)S(1)} async-done(((f32[2,1,256,1024]{3,0,1,2:T(2,128)}), f32[2,1,256,1024]{3,0,1,2:T(2,128)S(1)}, u32[]{:S(2)}, u32[]{:S(2)}) %all-to-all-start) | async-done | bytes 2097184 | tf_op jit(solution)/shard_map/all_to_all | solution.py:25
  71.1 0.7 copy.69
  71.7 6.5 %fusion.21 = f32[2,8,1024,64]{2,3,1,0:T(8,128)S(1)} fusion(f32[2,32,8,1024]{3,2,1,0:T(8,128)S(1)} %bitcast.172), kind=kOutput, calls=%fused_computation.40 | convolution fusion | flops 402681856 | bytes 6291456 | tf_op jit(solution)/shard_map/ks,gstc->gktc/dot_general | solution.py:29
  78.2 7.3 %fusion.2 = (f32[2,1,64,8,1024]{4,2,3,0,1:T(8,128)S(1)}, f32[2,1,64,8,1024]{4,2,3,0,1:T(8,128)S(1)}) fusion(f32[2,8,1024,64]{2,3,1,0:T(8,128)S(1)} %fusion.21, f32[64,8]{0,1:T(8,128)S(1)} %get-tuple-element.16, f32[64,8]{0,1:T(8,128)S(1)} %get-tuple-element.15, f32[2,32,8,1024]{3,2,1,0:T(8,128)S(1)} %bitcast.173), kind=kOutput, calls=%fused_computation.8 | convolution fusion | flops 410021888 | bytes 14684160 | tf_op jit(solution)/shard_map/ks,gstc->gktc/dot_general | solution.py:28
  85.6 14.2 %pad_maximum_fusion = f32[2,2,64,8,1024]{4,2,3,0,1:T(8,128)S(1)} fusion(f32[2,1,64,8,1024]{4,2,3,0,1:T(8,128)S(1)} %get-tuple-element.6, f32[2,1,64,8,1024]{4,2,3,0,1:T(8,128)S(1)} %get-tuple-element.5), kind=kLoop, calls=%fused_computation | loop fusion | flops 2097152 | bytes 16777216 | tf_op jit(solution)/shard_map/stack | solution.py:36
  99.8 8.1 %copy.39 = f32[2,2,64,8,1024]{4,3,0,1,2:T(8,128)} copy(f32[2,2,64,8,1024]{4,2,3,0,1:T(8,128)S(1)} %pad_maximum_fusion) | data formatting | bytes 16777216 | tf_op jit(solution)/shard_map/stack | solution.py:36
  107.9 5.4 all-to-all-start.1
  113.3 0.0 reduce-scatter.2.cloned.1.call-start
  113.4 0.1 fusion.110
  113.5 184.3 %all-to-all-done.1 = f32[2,2,64,8,1024]{4,3,0,1,2:T(8,128)} async-done(((f32[2,2,64,8,1024]{4,3,0,1,2:T(8,128)}), f32[2,2,64,8,1024]{4,3,0,1,2:T(8,128)}, u32[]{:S(2)}, u32[]{:S(2)}) %all-to-all-start.1) | async-done | bytes 8388640 | tf_op jit(solution)/shard_map/all_to_all | solution.py:37
  297.8 4.2 copy.67
  302.0 4.5 fusion.18
  306.4 4.4 fusion.14
  310.9 4.9 fusion.17
  315.8 4.5 fusion.13
  320.2 4.5 fusion.25
  324.8 4.7 fusion.27
  329.4 4.5 fusion.26
  334.0 5.2 multiply_subtract_fusion
  339.2 2.8 fusion.7
  342.0 2.8 fusion.5
  344.9 2.9 fusion.29
  347.8 3.2 subtract_bitcast_fusion
  350.9 2.4 pad_maximum_fusion.1
  353.4 7.4 %copy.46 = f32[2,2,256,1024]{3,1,0,2:T(2,128)} copy(f32[2,2,256,1024]{2,3,1,0:T(8,128)} %pad_maximum_fusion.1) | data formatting | bytes 8388608 | tf_op jit(solution)/shard_map/stack | solution.py:62
  360.8 100.3 %all_to_all.54 = f32[2,2,256,1024]{3,1,0,2:T(2,128)S(1)} all-to-all(f32[2,2,256,1024]{3,1,0,2:T(2,128)} %copy.46), channel_id=1, replica_groups=mesh['seq'=32,'tp'=8] {'seq'}, dimensions={2} | all-to-all | bytes 8388608 | tf_op jit(solution)/shard_map/all_to_all | solution.py:63
  461.1 2.4 copy.68
  463.6 1.8 fusion.175
  465.3 1.6 copy.48
  467.0 2.5 squeeze.25
  469.5 2.9 fusion.82
  472.4 2.9 copy.49
  475.3 2.7 squeeze.26
  478.0 1.2 fusion.35
  479.2 0.0 copy-start.2
  479.2 0.0 copy-start.3
  479.3 0.0 copy-start.4
  479.3 0.6 copy.50
  479.9 31.5 %all_to_all.55 = f32[32,8,1024]{2,1,0:T(8,128)S(1)} all-to-all(f32[32,8,1024]{2,1,0:T(8,128)S(1)} %copy.50), channel_id=1, replica_groups=mesh['seq'=32,'tp'=8] {'seq'}, dimensions={0} | all-to-all | bytes 2097152 | tf_op jit(solution)/shard_map/all_to_all | solution.py:73
  511.4 7.2 %fusion = bf16[4096,256]{0,1:T(8,128)(2,1)} fusion(bf16[1024,4096]{1,0:T(8,128)(2,1)} %param.11, f32[32,8,1024]{2,1,0:T(8,128)S(1)} %all_to_all.55, bf16[256,1024]{1,0:T(8,128)(2,1)S(1)} %copy-done.4, bf16[256,1024]{1,0:T(8,128)(2,1)S(1)} %copy-done.2, bf16[256,1024]{1,0:T(8,128)(2,1)S(1)} %copy-done.3, f32[1024]{0:T(1024)S(1)} %copy-done.5), kind=kOutput, calls=%fused_computation.3 | convolution fusion | flops 2150629376 | bytes 13111296 | tf_op jit(solution)/shard_map/dot_general | solution.py:78
  518.6 0.0 reduce-scatter.2.cloned.1.call-update
  518.7 92.5 %reduce-scatter.2.cloned.1.call-done = bf16[512,256]{0,1:T(8,128)(2,1)} async-done(((bf16[4096,256]{0,1:T(8,128)(2,1)}), bf16[512,256]{0,1:T(8,128)(2,1)}) %reduce-scatter.2.cloned.1.call-update) | async-done | bytes 262160 | tf_op jit(solution)/shard_map/reduce_scatter | solution.py:77
  (10 shorter events, 0.0 us)
Async XLA Ops:
  6.5 1.5 copy-start.1
  11.3 59.8 %all-to-all-start = ((f32[2,1,256,1024]{3,0,1,2:T(2,128)}), f32[2,1,256,1024]{3,0,1,2:T(2,128)S(1)}, u32[]{:S(2)}, u32[]{:S(2)}) async-start(f32[2,1,256,1024]{3,0,1,2:T(2,128)} %copy.35), calls=%async_computation | async-start | bytes 4194304 | tf_op jit(solution)/shard_map/all_to_all | solution.py:25
  107.9 189.9 %all-to-all-start.1 = ((f32[2,2,64,8,1024]{4,3,0,1,2:T(8,128)}), f32[2,2,64,8,1024]{4,3,0,1,2:T(8,128)}, u32[]{:S(2)}, u32[]{:S(2)}) async-start(f32[2,2,64,8,1024]{4,3,0,1,2:T(8,128)} %copy.39), calls=%async_computation.1 | async-start | bytes 16777216 | tf_op jit(solution)/shard_map/all_to_all | solution.py:37
  113.3 497.9 %reduce-scatter.2.cloned.1.call-start = ((), (), s32[]{:S(2)}) async-start(), calls=%async_computation.5 | async-start | bytes 2359296 | tf_op jit(solution)/shard_map/reduce_scatter | solution.py:77
  469.4 2.9 copy-start
  479.2 32.2 %copy-start.2 = (bf16[256,1024]{1,0:T(8,128)(2,1)S(1)}, bf16[256,1024]{1,0:T(8,128)(2,1)}, u32[]{:S(2)}) copy-start(bf16[256,1024]{1,0:T(8,128)(2,1)} %param.7) | copy-start | bytes 1572868
  479.2 32.2 %copy-start.3 = (bf16[256,1024]{1,0:T(8,128)(2,1)S(1)}, bf16[256,1024]{1,0:T(8,128)(2,1)}, u32[]{:S(2)}) copy-start(bf16[256,1024]{1,0:T(8,128)(2,1)} %param.6) | copy-start | bytes 1572868
  479.3 32.2 %copy-start.4 = (bf16[256,1024]{1,0:T(8,128)(2,1)S(1)}, bf16[256,1024]{1,0:T(8,128)(2,1)}, u32[]{:S(2)}) copy-start(bf16[256,1024]{1,0:T(8,128)(2,1)} %param.8) | copy-start | bytes 1572868
  479.3 32.2 %copy-start.5 = (f32[1024]{0:T(1024)S(1)}, f32[1024]{0:T(1024)}, u32[]{:S(2)}) copy-start(f32[1024]{0:T(1024)} %param.10) | copy-start | bytes 12292
Sparse Core Ops, SparseCore 0:
  518.8 92.3 reduce-scatter.1
where the time goes:
time: 622 us; the launch traced here: 618 us
  waiting for transfers between devices  326 us (52%)
  blocking collectives  132 us (21%)
  matrix products  74 us (12%)
  local copies, waits for them, and re-layouts  38.1 us (6%)
  other arithmetic  18.5 us (3%)
  starting transfers between devices  15.9 us (3%)
  between operations  13.9 us (2%)
    all_to_all x1, waiting for transfers between devices, local(): lax.all_to_all(spread, 'seq', split_axis=2, concat_axis=3, tiled=True)  184 us
    all_to_all x1, blocking collectives, local(): lax.all_to_all(spectra, 'seq', split_axis=2, concat_axis=1, tiled=True)  100 us
    reduce_scatter x1, waiting for transfers between devices, local(): lax.psum_scatter(lax.dot_general(w_out, mixed, (((0,), (1,)), ((), ())),...  92.5 us
    all_to_all x1, waiting for transfers between devices, local(): lax.all_to_all(paired, 'seq', split_axis=2, concat_axis=1, tiled=True)  49.2 us
    dot_general x12, matrix products, apply(): return jnp.einsum('kt,jtc->jkc', table, operand, precision=HIGH)  48.9 us
    all_to_all x1, blocking collectives, local(): lax.all_to_all(moved, 'seq', split_axis=0, concat_axis=1, tiled=True)[0]  31.5 us
    another operation x1, other arithmetic, local(): spread = jnp.stack([out_real, out_imag], axis=1)  14.2 us
  transfers between devices with their start and end apart: 3, of which 3 were waited for; matrix products, arithmetic and copies ran while one was open for 0% of the time, Pallas kernels for 0%

commit v1 on v0

v1 whole, which is shorter than its diff:
```python
import math

import jax
import jax.numpy as jnp
import numpy as np
from jax import lax
from jax.experimental import pallas as pl
from jax.experimental.pallas import tpu as pltpu
from jax.sharding import PartitionSpec as P

MESH = pl.DeviceIdType.MESH
NT = (((1,), (1,)), ((), ()))
SEQ = 32
CHAN = 32
FINE = 256
BINS = 33
LENGTH = 2 * SEQ * FINE


def twist(z, angle):
    c, s = math.cos(angle), math.sin(angle)
    re, im = z
    if abs(s) < 1e-9:
        return (re, im) if c > 0 else (-re, -im)
    if abs(c) < 1e-9:
        return (-im, re) if s > 0 else (im, -re)
    if abs(abs(c) - abs(s)) < 1e-9:
        a = abs(c)
        d, e = (re - im) * a, (re + im) * a
        if c > 0:
            return (d, e) if s > 0 else (e, -d)
        return (-e, d) if s > 0 else (-d, -e)
    return (re * c - im * s, re * s + im * c)


def cadd(a, b):
    return (a[0] + b[0], a[1] + b[1])


def csub(a, b):
    return (a[0] - b[0], a[1] - b[1])


def complex_dft(z, sign):
    n = len(z)
    if n == 1:
        return z
    even, odd = complex_dft(z[0::2], sign), complex_dft(z[1::2], sign)
    first, second = [], []
    for k in range(n // 2):
        t = twist(odd[k], sign * 2 * math.pi * k / n)
        first.append(cadd(even[k], t))
        second.append(csub(even[k], t))
    return first + second


def odd_bins(v):
    n = 2 * len(v)
    q = n // 4
    z = [twist((v[p], -v[p + q]), -2 * math.pi * p / n) for p in range(q)]
    bins = {}
    for r, value in enumerate(complex_dft(z, -1)):
        k = 4 * r + 1
        bins[k if k <= n // 2 else n - k] = value if k <= n // 2 else (value[0], -value[1])
    return bins


def real_dft(x):
    n = len(x)
    if n == 2:
        return {0: (x[0] + x[1], None), 1: (x[0] - x[1], None)}
    h = n // 2
    bins = {2 * k: value for k, value in real_dft([x[p] + x[p + h] for p in range(h)]).items()}
    bins.update(odd_bins([x[p] - x[p + h] for p in range(h)]))
    return bins


def padded_real_dft(x):
    bins = {2 * k: value for k, value in real_dft(x).items()}
    bins.update(odd_bins(x))
    return bins


def odd_back(bins, n):
    q = n // 4
    z = []
    for r in range(q):
        k = 4 * r + 1
        z.append(bins[k] if k <= n // 2 else (bins[n - k][0], -bins[n - k][1]))
    d = [twist(c, 2 * math.pi * p / n) for p, c in enumerate(complex_dft(z, 1))]
    return [a for a, _ in d] + [-b for _, b in d]


def real_back(bins, n):
    if n == 2:
        return [bins[0][0] + bins[1][0], bins[0][0] - bins[1][0]]
    u = real_back({k // 2: value for k, value in bins.items() if k % 2 == 0}, n // 2)
    v = odd_back(bins, n)
    return [a + b for a, b in zip(u, v)] + [a - b for a, b in zip(u, v)]


def half_real_back(bins, n):
    u = real_back({k // 2: value for k, value in bins.items() if k % 2 == 0}, n // 2)
    return [a + b for a, b in zip(u, odd_back(bins, n))]


def tables():
    idx = np.arange(FINE)
    ang = 2 * np.pi * ((idx[:, None] * idx[None, :]) % FINE) / FINE
    c, s = np.cos(ang), np.sin(ang)
    forward = np.block([[c, -s], [s, c]])
    back = np.block([[c, s], [-s, c]])
    tw = 2 * np.pi * np.arange(BINS)[:, None] * idx[None, :] / LENGTH
    scale = np.full((BINS, 1), 2.0 / LENGTH)
    scale[0] = scale[-1] = 1.0 / LENGTH
    twiddle = np.stack([np.cos(tw), np.sin(tw), np.cos(tw) * scale, np.sin(tw) * scale], 1)
    return (
        jnp.asarray(forward, jnp.bfloat16),
        jnp.asarray(back, jnp.bfloat16),
        jnp.asarray(twiddle, jnp.float32),
    )


def identity():
    row = lax.broadcasted_iota(jnp.int32, (FINE, FINE), 0)
    col = lax.broadcasted_iota(jnp.int32, (FINE, FINE), 1)
    return jnp.where(row == col, 1.0, 0.0).astype(jnp.bfloat16)


def spread_kernel(inner, values, filters, recv, send, eye, send_sem, recv_sem):
    me = lax.axis_index("seq")
    barrier = pltpu.get_barrier_semaphore()

    @pl.loop(1, SEQ)
    def _(i):
        pl.semaphore_signal(barrier, inc=1, device_id={"seq": me ^ i}, device_id_type=MESH)

    eye[...] = identity()
    pl.semaphore_wait(barrier, SEQ - 1)

    @pl.loop(0, 4)
    def _(step):
        block = lax.rem(me // 8 + 1 + step, 4)
        cols = pl.ds(pl.multiple_of(block * FINE, FINE), FINE)
        product = (inner[:, cols].astype(jnp.float32) * values[:, cols].astype(jnp.float32)).astype(jnp.bfloat16)
        for half, part in enumerate((product, filters[:, cols].astype(jnp.bfloat16))):
            turned = lax.dot_general(eye[...], part, NT, preferred_element_type=jnp.float32)
            send[pl.ds(block * 8, 8), half * CHAN : (half + 1) * CHAN, :] = turned.astype(jnp.bfloat16).reshape(8, CHAN, FINE)

        @pl.loop(0, 8)
        def _(i):
            peer = block * 8 + (lax.rem(me, 8) ^ (7 - i))

            @pl.when(peer != me)
            def _():
                pltpu.make_async_remote_copy(
                    send.at[peer], recv.at[me], send_sem, recv_sem, device_id={"seq": peer}, device_id_type=MESH
                ).start()

    recv[me] = send[me]
    pltpu.make_async_copy(send.at[pl.ds(0, SEQ - 1)], send.at[pl.ds(0, SEQ - 1)], send_sem).wait()
    pltpu.make_async_copy(recv.at[pl.ds(0, SEQ - 1)], recv.at[pl.ds(0, SEQ - 1)], recv_sem).wait()


def spread(inner, values, filters):
    vmem = pl.BlockSpec(memory_space=pltpu.VMEM)
    return pl.pallas_call(
        spread_kernel,
        out_shape=jax.ShapeDtypeStruct((SEQ, 2 * CHAN, FINE), jnp.bfloat16),
        in_specs=[vmem] * 3,
        out_specs=vmem,
        scratch_shapes=[
            pltpu.VMEM((SEQ, 2 * CHAN, FINE), jnp.bfloat16),
            pltpu.VMEM((FINE, FINE), jnp.bfloat16),
            pltpu.SemaphoreType.DMA,
            pltpu.SemaphoreType.DMA,
        ],
        compiler_params=pltpu.CompilerParams(collective_id=0, has_side_effects=True, vmem_limit_bytes=40 * 2**20),
        name="spread",
    )(inner, values, filters)


def conv_kernel(block, forward, back, twiddle, out, spec, waves):
    f32 = jnp.float32

    @pl.loop(0, 4)
    def _(group):
        rows = pl.ds(pl.multiple_of(group * 16, 16), 16)
        for lane in range(2):
            lanes = slice(lane * 128, lane * 128 + 128)
            bins = padded_real_dft([block[p, rows, lanes].astype(f32) for p in range(SEQ)])
            for k, (re, im) in bins.items():
                c, s = twiddle[k, 0:1, lanes], twiddle[k, 1:2, lanes]
                if im is None:
                    a, b = re * c, -(re * s)
                else:
                    a, b = re * c + im * s, im * c - re * s
                spec[k, rows, lanes] = a.astype(jnp.bfloat16)
                spec[k, rows, lane * 128 + FINE : lane * 128 + FINE + 128] = b.astype(jnp.bfloat16)

    group_bins = 11

    @pl.loop(0, BINS // group_bins)
    def _(step):
        at = pl.ds(step * group_bins, group_bins)
        both = jnp.dot(
            spec[at].reshape(group_bins * 2 * CHAN, 2 * FINE), forward[...], preferred_element_type=f32
        ).reshape(group_bins, 2, CHAN, 2 * FINE)
        zr, zi = both[:, 0, :, :FINE], both[:, 0, :, FINE:]
        hr, hi = both[:, 1, :, :FINE], both[:, 1, :, FINE:]
        y = jnp.concatenate([zr * hr - zi * hi, zr * hi + zi * hr], axis=-1).astype(jnp.bfloat16)
        waves[at] = jnp.dot(
            y.reshape(group_bins * CHAN, 2 * FINE), back[...], preferred_element_type=f32
        ).reshape(group_bins, CHAN, 2 * FINE)

    @pl.loop(0, 2)
    def _(group):
        rows = pl.ds(pl.multiple_of(group * 16, 16), 16)
        for lane in range(2):
            lanes = slice(lane * 128, lane * 128 + 128)
            bins = {}
            for k in range(BINS):
                re, im = waves[k, rows, lanes], waves[k, rows, lane * 128 + FINE : lane * 128 + FINE + 128]
                c, s = twiddle[k, 2:3, lanes], twiddle[k, 3:4, lanes]
                bins[k] = (re * c - im * s, None if k in (0, BINS - 1) else im * c + re * s)
            for p, y in enumerate(half_real_back(bins, 2 * SEQ)):
                out[p, rows, lanes] = y.astype(jnp.bfloat16)


def convolve(block):
    vmem = pl.BlockSpec(memory_space=pltpu.VMEM)
    return pl.pallas_call(
        conv_kernel,
        out_shape=jax.ShapeDtypeStruct((SEQ, CHAN, FINE), jnp.bfloat16),
        in_specs=[vmem] * 4,
        out_specs=vmem,
        scratch_shapes=[
            pltpu.VMEM((BINS, 2 * CHAN, 2 * FINE), jnp.bfloat16),
            pltpu.VMEM((BINS, CHAN, 2 * FINE), jnp.float32),
        ],
        compiler_params=pltpu.CompilerParams(vmem_limit_bytes=40 * 2**20),
        name="convolve",
    )(block, *tables())


def project_kernel(
    conv, inner, values, outer, skip, w_hbm, out,
    turned, mixed, eye, w, psend, precv, kept, zsend, zrecv,
    w_sem, send_sem, recv_sem, psend_sem, precv_sem, zsend_sem, zrecv_sem,
):
    f32 = jnp.float32
    me, tp = lax.axis_index("seq"), lax.axis_index("tp")
    y, z = tp // 2, lax.rem(tp, 2)
    load = pltpu.make_async_copy(w_hbm, w, w_sem)
    load.start()
    barrier = pltpu.get_barrier_semaphore()

    @pl.loop(1, SEQ)
    def _(i):
        pl.semaphore_signal(barrier, inc=1, device_id={"seq": me ^ i}, device_id_type=MESH)

    for d in range(1, 4):
        pl.semaphore_signal(barrier, inc=1, device_id={"tp": lax.rem(y + d, 4) * 2 + z}, device_id_type=MESH)
    pl.semaphore_signal(barrier, inc=1, device_id={"tp": y * 2 + 1 - z}, device_id_type=MESH)
    eye[...] = identity()
    pl.semaphore_wait(barrier, SEQ + 3)

    @pl.loop(1, SEQ)
    def _(i):
        peer = me ^ (SEQ - i)
        pltpu.make_async_remote_copy(
            conv.at[peer], turned.at[me], send_sem, recv_sem, device_id={"seq": peer}, device_id_type=MESH
        ).start()

    turned[me] = conv[me]
    pltpu.make_async_copy(conv.at[pl.ds(0, SEQ - 1)], conv.at[pl.ds(0, SEQ - 1)], send_sem).wait()
    pltpu.make_async_copy(turned.at[pl.ds(0, SEQ - 1)], turned.at[pl.ds(0, SEQ - 1)], recv_sem).wait()

    @pl.loop(0, 4)
    def _(block):
        cols = pl.ds(pl.multiple_of(block * FINE, FINE), FINE)
        part = turned[pl.ds(block * 8, 8)].reshape(FINE, FINE)
        here = lax.dot_general(eye[...], part, NT, preferred_element_type=f32)
        product = inner[:, cols].astype(f32) * values[:, cols].astype(f32)
        mixed[:, cols] = (outer[:, cols].astype(f32) * (here + skip[:, cols] * product)).astype(jnp.bfloat16)

    load.wait()

    def shares(chunk, d):
        target = lax.rem(y + d, 4)
        return pltpu.make_async_remote_copy(
            psend.at[chunk, d], precv.at[chunk, d], psend_sem.at[chunk, d], precv_sem.at[chunk, d],
            device_id={"tp": target * 2 + z}, device_id_type=MESH,
        )

    def swap(chunk):
        return pltpu.make_async_remote_copy(
            zsend.at[chunk], zrecv.at[chunk], zsend_sem.at[chunk], zrecv_sem.at[chunk],
            device_id={"tp": y * 2 + 1 - z}, device_id_type=MESH,
        )

    for chunk in range(2):
        rows = slice(chunk * 128, chunk * 128 + 128)
        for d in (2, 1, 3, 0):
            target = lax.rem(y + d, 4)

            @pl.loop(0, 2)
            def _(part):
                cols = pl.ds(pl.multiple_of(target * 1024 + part * 512, 512), 512)
                psend[chunk, d, :, pl.ds(pl.multiple_of(part * 512, 512), 512)] = jnp.dot(
                    mixed[rows, :], w[:, cols], preferred_element_type=f32
                ).astype(jnp.bfloat16)

            if d:
                shares(chunk, d).start()

    for chunk in range(2):
        for d in range(1, 4):
            shares(chunk, d).wait_recv()

        def total(half):
            cols = pl.ds(pl.multiple_of(half * 512, 512), 512)
            acc = psend[chunk, 0, :, cols].astype(f32)
            for d in range(1, 4):
                acc += precv[chunk, d, :, cols].astype(f32)
            return acc

        zsend[chunk] = total(1 - z).astype(jnp.bfloat16)
        swap(chunk).start()
        kept[chunk] = total(z)

    for chunk in range(2):
        swap(chunk).wait()
        out[chunk * 128 : chunk * 128 + 128, :] = (kept[chunk] + zrecv[chunk].astype(f32)).astype(jnp.bfloat16)
        for d in range(1, 4):
            shares(chunk, d).wait_send()


def project(conv, inner, values, outer, skip, w_out):
    vmem = pl.BlockSpec(memory_space=pltpu.VMEM)
    bf16 = jnp.bfloat16
    return pl.pallas_call(
        project_kernel,
        out_shape=jax.ShapeDtypeStruct((FINE, 512), bf16),
        in_specs=[vmem] * 5 + [pl.BlockSpec(memory_space=pl.ANY)],
        out_specs=vmem,
        scratch_shapes=[
            pltpu.VMEM((SEQ, CHAN, FINE), bf16),
            pltpu.VMEM((FINE, 1024), bf16),
            pltpu.VMEM((FINE, FINE), bf16),
            pltpu.VMEM((1024, 4096), bf16),
            pltpu.VMEM((2, 4, 128, 1024), bf16),
            pltpu.VMEM((2, 4, 128, 1024), bf16),
            pltpu.VMEM((2, 128, 512), jnp.float32),
            pltpu.VMEM((2, 128, 512), bf16),
            pltpu.VMEM((2, 128, 512), bf16),
            pltpu.SemaphoreType.DMA,
            pltpu.SemaphoreType.DMA,
            pltpu.SemaphoreType.DMA,
            pltpu.SemaphoreType.DMA((2, 4)),
            pltpu.SemaphoreType.DMA((2, 4)),
            pltpu.SemaphoreType.DMA((2,)),
            pltpu.SemaphoreType.DMA((2,)),
        ],
        compiler_params=pltpu.CompilerParams(collective_id=1, has_side_effects=True, vmem_limit_bytes=50 * 2**20),
        name="project",
    )(conv, inner, values, outer, skip.reshape(1, -1), w_out)


def local(inner_gate, values, outer_gate, filters, skip_gain, w_out):
    block = spread(inner_gate, values, filters)
    conv = convolve(block)
    return project(conv, inner_gate, values, outer_gate, skip_gain, w_out)


def solution(mesh):
    in_specs = (P("seq", "tp"), P("seq", "tp"), P("seq", "tp"), P("seq", "tp"), P("tp"), P("tp", None))
    return jax.shard_map(local, mesh=mesh, in_specs=in_specs, out_specs=P("seq", "tp"), check_vma=False)
```

time: 622 us -> 104 us (0.17)
  waiting for transfers between devices: 326 us -> 0 us
  blocking collectives: 132 us -> 0 us
  Pallas kernels: 0 us -> 92.5 us
  matrix products: 74 us -> 0 us
  local copies, waits for them, and re-layouts: 38.1 us -> 10.8 us
  other arithmetic: 18.5 us -> 0 us
  starting transfers between devices: 15.9 us -> 0 us
  between operations: 13.9 us -> 0.05 us
    all_to_all x2 -> x0, waiting for transfers between devices: 234 us -> none  [the longest x1 184 us: local(): lax.all_to_all(spread, 'seq', split_axis=2, concat_axis=3, tiled=True)]
    all_to_all x2 -> x0, blocking collectives: 132 us -> none  [the longest x1 100 us: local(): lax.all_to_all(spectra, 'seq', split_axis=2, concat_axis=1, tiled=True)]
    reduce_scatter x1 -> x0, waiting for transfers between devices: 92.5 us -> none  [local(): lax.psum_scatter(lax.dot_general(w_out, mixed, (((0,), (1,)), ((), ())),...]
    pallas_call x0 -> x3, Pallas kernels: none -> 92.5 us  [the longest x1 54.7 us: project(): pl.pallas_call(project_kernel, out_shape=jax.ShapeDtypeStruct((FINE, 512)...]
    dot_general x17 -> x0, matrix products: 74 us -> none  [the longest x12 48.9 us: apply(): return jnp.einsum('kt,jtc->jkc', table, operand, precision=HIGH)]
    another operation x3 -> x0, other arithmetic: 18 us -> none  [the longest x1 14.2 us: local(): spread = jnp.stack([out_real, out_imag], axis=1)]
    all_to_all x2 -> x0, starting transfers between devices: 15.8 us -> none  [the longest x1 10.4 us: local(): lax.all_to_all(paired, 'seq', split_axis=2, concat_axis=1, tiled=True)]
    another operation x2 -> x0, local copies, waits for them, and re-layouts: 15.5 us -> none  [the longest x1 8.1 us: local(): spread = jnp.stack([out_real, out_imag], axis=1)]
  transfers between devices with their start and end apart: 3 -> 0, of which waited for: 3 -> 0; matrix products, arithmetic and copies ran while one was open for 0% -> 0% of each run, Pallas kernels for 0% -> 0%
where the time goes in v1:
time: 104 us; the launch traced here: 103 us
  Pallas kernels  92.5 us (89%)
  local copies, waits for them, and re-layouts  10.8 us (10%)
    pallas_call x1, Pallas kernels, project(): pl.pallas_call(project_kernel, out_shape=jax.ShapeDtypeStruct((FINE, 512)...  54.7 us
    pallas_call x1, Pallas kernels, spread(): pl.pallas_call(spread_kernel, out_shape=jax.ShapeDtypeStruct((SEQ, 2 * CH...  32.6 us
    unnamed x21, local copies, waits for them, and re-layouts  10.8 us
    pallas_call x1, Pallas kernels, convolve(): pl.pallas_call(conv_kernel, out_shape=jax.ShapeDtypeStruct((SEQ, CHAN, FI...  5.18 us

profile of v1, /device:TPU:1, one launch (start us, length us, event | category | flops | bytes accessed | tf_op | source)
XLA Modules:
  0.0 103.3 jit_solution(9836095745340033998)
XLA Ops:
  0.0 0.0 copy-start
  0.0 1.0 %copy-done = bf16[256,1024]{1,0:T(8,128)(2,1)S(1)} copy-done((bf16[256,1024]{1,0:T(8,128)(2,1)S(1)}, bf16[256,1024]{1,0:T(8,128)(2,1)}, u32[]{:S(2)}) %copy-start) | copy-done | bytes 524312
  1.0 0.0 copy-start.2
  1.0 1.0 %copy-done.2 = bf16[256,1024]{1,0:T(8,128)(2,1)S(1)} copy-done((bf16[256,1024]{1,0:T(8,128)(2,1)S(1)}, bf16[256,1024]{1,0:T(8,128)(2,1)}, u32[]{:S(2)}) %copy-start.2) | copy-done | bytes 524312
  2.1 0.0 copy-start.4
  2.1 1.2 %copy-done.4 = f32[256,1024]{1,0:T(8,128)S(1)} copy-done((f32[256,1024]{1,0:T(8,128)S(1)}, f32[256,1024]{1,0:T(8,128)}, u32[]{:S(2)}) %copy-start.4) | copy-done | bytes 1048600
  3.3 32.6 %spread.1.block = bf16[32,64,256]{2,1,0:T(8,128)(2,1)S(1)} custom-call(bf16[256,1024]{1,0:T(8,128)(2,1)S(1)} %copy-done, bf16[256,1024]{1,0:T(8,128)(2,1)S(1)} %copy-done.2, f32[256,1024]{1,0:T(8,128)S(1)} %copy-done.4), custom_call_target="tpu_custom_call" | custom-call | tf_op jit(solution)/shard_map/spread/pallas_call | solution.py:167
  35.9 0.0 copy-start.6
  35.9 1.0 copy-done.6
  37.0 0.0 copy-start.7
  37.0 1.0 %copy-done.7 = bf16[512,512]{1,0:T(8,128)(2,1)S(1)} copy-done((bf16[512,512]{1,0:T(8,128)(2,1)S(1)}, bf16[512,512]{1,0:T(8,128)(2,1)}, u32[]{:S(2)}) %copy-start.7) | copy-done | bytes 524312
  38.0 0.0 copy-start.8
  38.0 0.9 copy-done.8
  38.9 5.2 %convolve.1.conv = bf16[32,32,256]{2,1,0:T(8,128)(2,1)S(1)} custom-call(bf16[32,64,256]{2,1,0:T(8,128)(2,1)S(1)} %spread.1.block, bf16[512,512]{1,0:T(8,128)(2,1)S(1)} %copy-done.7, bf16[512,512]{1,0:T(8,128)(2,1)S(1)} %copy-done.6, f32[33,4,256]{2,1,0:T(4,128)S(1)} %copy-done.8), custom_call_target="tpu_custom_call" | custom-call | tf_op jit(solution)/shard_map/convolve/pallas_call | solution.py:232
  44.1 0.0 copy-start.1
  44.1 1.0 copy-done.1
  45.1 0.0 copy-start.3
  45.1 1.0 %copy-done.3 = bf16[256,1024]{1,0:T(8,128)(2,1)S(1)} copy-done((bf16[256,1024]{1,0:T(8,128)(2,1)S(1)}, bf16[256,1024]{1,0:T(8,128)(2,1)}, u32[]{:S(2)}) %copy-start.3) | copy-done | bytes 524312
  46.2 0.0 copy-start.5
  46.2 1.0 %copy-done.5 = bf16[256,1024]{1,0:T(8,128)(2,1)S(1)} copy-done((bf16[256,1024]{1,0:T(8,128)(2,1)S(1)}, bf16[256,1024]{1,0:T(8,128)(2,1)}, u32[]{:S(2)}) %copy-start.5) | copy-done | bytes 524312
  47.2 0.0 copy-start.9
  47.2 0.7 copy-done.9
  47.9 54.7 %project.1 = bf16[256,512]{1,0:T(8,128)(2,1)S(1)} custom-call(bf16[32,32,256]{2,1,0:T(8,128)(2,1)S(1)} %convolve.1.conv, bf16[256,1024]{1,0:T(8,128)(2,1)S(1)} %copy-done.1, bf16[256,1024]{1,0:T(8,128)(2,1)S(1)} %copy-done.3, bf16[256,1024]{1,0:T(8,128)(2,1)S(1)} %copy-done.5, f32[1,1024]{1,0:T(1,128)S(1)} %bitcast.1, bf16[1024,4096]{1,0:T(8,128)(2,1)} %w_hbm.1), custom_call_target="tpu_custom_call" | custom-call | tf_op jit(solution)/shard_map/project/pallas_call | solution.py:342
  102.6 0.7 copy.11
Async XLA Ops:
  0.0 1.0 %copy-start = (bf16[256,1024]{1,0:T(8,128)(2,1)S(1)}, bf16[256,1024]{1,0:T(8,128)(2,1)}, u32[]{:S(2)}) copy-start(bf16[256,1024]{1,0:T(8,128)(2,1)} %inner.3) | copy-start | bytes 1572868
  1.0 1.0 %copy-start.2 = (bf16[256,1024]{1,0:T(8,128)(2,1)S(1)}, bf16[256,1024]{1,0:T(8,128)(2,1)}, u32[]{:S(2)}) copy-start(bf16[256,1024]{1,0:T(8,128)(2,1)} %values.3) | copy-start | bytes 1572868
  2.1 1.2 %copy-start.4 = (f32[256,1024]{1,0:T(8,128)S(1)}, f32[256,1024]{1,0:T(8,128)}, u32[]{:S(2)}) copy-start(f32[256,1024]{1,0:T(8,128)} %filters.1) | copy-start | bytes 3145732
  35.9 1.0 %copy-start.6 = (bf16[512,512]{1,0:T(8,128)(2,1)S(1)}, bf16[512,512]{1,0:T(8,128)(2,1)}, u32[]{:S(2)}) copy-start(bf16[512,512]{1,0:T(8,128)(2,1)} %constant.7.clone.back) | copy-start | bytes 1572868
  37.0 1.0 %copy-start.7 = (bf16[512,512]{1,0:T(8,128)(2,1)S(1)}, bf16[512,512]{1,0:T(8,128)(2,1)}, u32[]{:S(2)}) copy-start(bf16[512,512]{1,0:T(8,128)(2,1)} %constant.6.clone.forward) | copy-start | bytes 1572868
  38.0 0.9 copy-start.8
  44.1 1.0 %copy-start.1 = (bf16[256,1024]{1,0:T(8,128)(2,1)S(1)}, bf16[256,1024]{1,0:T(8,128)(2,1)}, u32[]{:S(2)}) copy-start(bf16[256,1024]{1,0:T(8,128)(2,1)} %inner.3) | copy-start | bytes 1572868
  45.1 1.0 %copy-start.3 = (bf16[256,1024]{1,0:T(8,128)(2,1)S(1)}, bf16[256,1024]{1,0:T(8,128)(2,1)}, u32[]{:S(2)}) copy-start(bf16[256,1024]{1,0:T(8,128)(2,1)} %values.3) | copy-start | bytes 1572868
  46.2 1.0 %copy-start.5 = (bf16[256,1024]{1,0:T(8,128)(2,1)S(1)}, bf16[256,1024]{1,0:T(8,128)(2,1)}, u32[]{:S(2)}) copy-start(bf16[256,1024]{1,0:T(8,128)(2,1)} %outer.1) | copy-start | bytes 1572868
  47.2 0.7 copy-start.9

commit v2 on v1

v2 whole, which is shorter than its diff:
```python
import math

import jax
import jax.numpy as jnp
import numpy as np
from jax import lax
from jax.experimental import pallas as pl
from jax.experimental.pallas import tpu as pltpu
from jax.sharding import PartitionSpec as P

MESH = pl.DeviceIdType.MESH
NT = (((1,), (1,)), ((), ()))
SEQ = 32
PART = 16
FINE = 256
BINS = 33
LENGTH = 2 * SEQ * FINE


def twist(z, angle):
    c, s = math.cos(angle), math.sin(angle)
    re, im = z
    if abs(s) < 1e-9:
        return (re, im) if c > 0 else (-re, -im)
    if abs(c) < 1e-9:
        return (-im, re) if s > 0 else (im, -re)
    if abs(abs(c) - abs(s)) < 1e-9:
        a = abs(c)
        d, e = (re - im) * a, (re + im) * a
        if c > 0:
            return (d, e) if s > 0 else (e, -d)
        return (-e, d) if s > 0 else (-d, -e)
    return (re * c - im * s, re * s + im * c)


def cadd(a, b):
    return (a[0] + b[0], a[1] + b[1])


def csub(a, b):
    return (a[0] - b[0], a[1] - b[1])


def complex_dft(z, sign):
    n = len(z)
    if n == 1:
        return z
    even, odd = complex_dft(z[0::2], sign), complex_dft(z[1::2], sign)
    first, second = [], []
    for k in range(n // 2):
        t = twist(odd[k], sign * 2 * math.pi * k / n)
        first.append(cadd(even[k], t))
        second.append(csub(even[k], t))
    return first + second


def odd_bins(v):
    n = 2 * len(v)
    q = n // 4
    z = [twist((v[p], -v[p + q]), -2 * math.pi * p / n) for p in range(q)]
    bins = {}
    for r, value in enumerate(complex_dft(z, -1)):
        k = 4 * r + 1
        bins[k if k <= n // 2 else n - k] = value if k <= n // 2 else (value[0], -value[1])
    return bins


def real_dft(x):
    n = len(x)
    if n == 2:
        return {0: (x[0] + x[1], None), 1: (x[0] - x[1], None)}
    h = n // 2
    bins = {2 * k: value for k, value in real_dft([x[p] + x[p + h] for p in range(h)]).items()}
    bins.update(odd_bins([x[p] - x[p + h] for p in range(h)]))
    return bins


def padded_real_dft(x):
    bins = {2 * k: value for k, value in real_dft(x).items()}
    bins.update(odd_bins(x))
    return bins


def odd_back(bins, n):
    q = n // 4
    z = []
    for r in range(q):
        k = 4 * r + 1
        z.append(bins[k] if k <= n // 2 else (bins[n - k][0], -bins[n - k][1]))
    d = [twist(c, 2 * math.pi * p / n) for p, c in enumerate(complex_dft(z, 1))]
    return [a for a, _ in d] + [-b for _, b in d]


def real_back(bins, n):
    if n == 2:
        return [bins[0][0] + bins[1][0], bins[0][0] - bins[1][0]]
    u = real_back({k // 2: value for k, value in bins.items() if k % 2 == 0}, n // 2)
    v = odd_back(bins, n)
    return [a + b for a, b in zip(u, v)] + [a - b for a, b in zip(u, v)]


def half_real_back(bins, n):
    u = real_back({k // 2: value for k, value in bins.items() if k % 2 == 0}, n // 2)
    return [a + b for a, b in zip(u, odd_back(bins, n))]


def tables():
    idx = np.arange(FINE)
    ang = 2 * np.pi * ((idx[:, None] * idx[None, :]) % FINE) / FINE
    c, s = np.cos(ang), np.sin(ang)
    forward = np.block([[c, -s], [s, c]])
    back = np.block([[c, s], [-s, c]])
    tw = 2 * np.pi * np.arange(BINS)[:, None] * idx[None, :] / LENGTH
    scale = np.full((BINS, 1), 2.0 / LENGTH)
    scale[0] = scale[-1] = 1.0 / LENGTH
    twiddle = np.stack([np.cos(tw), np.sin(tw), np.cos(tw) * scale, np.sin(tw) * scale], 1)
    return (
        jnp.asarray(forward, jnp.bfloat16),
        jnp.asarray(back, jnp.bfloat16),
        jnp.asarray(twiddle, jnp.float32),
    )


def identity():
    row = lax.broadcasted_iota(jnp.int32, (FINE, FINE), 0)
    col = lax.broadcasted_iota(jnp.int32, (FINE, FINE), 1)
    return jnp.where(row == col, 1.0, 0.0).astype(jnp.bfloat16)


def transform(part, recv, forward, back, twiddle, spec, waves, conv):
    f32 = jnp.float32
    bf16 = jnp.bfloat16
    for kind in range(2):
        for lane in range(2):
            lanes = slice(lane * 128, lane * 128 + 128)
            bins = padded_real_dft([recv[part, p, kind, :, lanes].astype(f32) for p in range(SEQ)])
            for k, (re, im) in bins.items():
                c, s = twiddle[k, 0:1, lanes], twiddle[k, 1:2, lanes]
                if im is None:
                    a, b = re * c, -(re * s)
                else:
                    a, b = re * c + im * s, im * c - re * s
                spec[k, kind, :, lanes] = a.astype(bf16)
                spec[k, kind, :, lane * 128 + FINE : lane * 128 + FINE + 128] = b.astype(bf16)

    group = 11

    @pl.loop(0, BINS // group)
    def _(step):
        at = pl.ds(step * group, group)
        both = jnp.dot(
            spec[at].reshape(group * 2 * PART, 2 * FINE), forward[...], preferred_element_type=f32
        ).reshape(group, 2, PART, 2 * FINE)
        zr, zi = both[:, 0, :, :FINE], both[:, 0, :, FINE:]
        hr, hi = both[:, 1, :, :FINE], both[:, 1, :, FINE:]
        y = jnp.concatenate([zr * hr - zi * hi, zr * hi + zi * hr], axis=-1).astype(bf16)
        waves[at] = jnp.dot(y.reshape(group * PART, 2 * FINE), back[...], preferred_element_type=f32).reshape(
            group, PART, 2 * FINE
        )

    for lane in range(2):
        lanes = slice(lane * 128, lane * 128 + 128)
        bins = {}
        for k in range(BINS):
            re, im = waves[k, :, lanes], waves[k, :, lane * 128 + FINE : lane * 128 + FINE + 128]
            c, s = twiddle[k, 2:3, lanes], twiddle[k, 3:4, lanes]
            bins[k] = (re * c - im * s, None if k in (0, BINS - 1) else im * c + re * s)
        for p, y in enumerate(half_real_back(bins, 2 * SEQ)):
            conv[lane, part, p] = y.astype(bf16)


def kernel(
    inner_hbm, values_hbm, outer_hbm, filters_hbm, skip_hbm, w_hbm, forward_hbm, back_hbm, twiddle_hbm, out,
    inner, values, outer, filters, skip, w, forward, back, twiddle,
    send, recv, spec, waves, conv, turned, mixed, eye, psend, precv, kept, zsend, zrecv,
    load_sem, send_sem, recv_sem, csend_sem, crecv_sem, psend_sem, precv_sem, zsend_sem, zrecv_sem,
):
    f32 = jnp.float32
    bf16 = jnp.bfloat16
    me, tp = lax.axis_index("seq"), lax.axis_index("tp")
    y, z = tp // 2, lax.rem(tp, 2)
    loads = [
        pltpu.make_async_copy(a, b, load_sem.at[i])
        for i, (a, b) in enumerate((
            (inner_hbm, inner), (values_hbm, values), (filters_hbm, filters), (forward_hbm, forward), (back_hbm, back),
            (twiddle_hbm, twiddle), (outer_hbm, outer), (skip_hbm, skip), (w_hbm, w),
        ))
    ]
    for load in loads:
        load.start()
    barrier = pltpu.get_barrier_semaphore()

    @pl.loop(1, SEQ)
    def _(i):
        pl.semaphore_signal(barrier, inc=1, device_id={"seq": me ^ i}, device_id_type=MESH)

    for d in range(1, 4):
        pl.semaphore_signal(barrier, inc=1, device_id={"tp": lax.rem(y + d, 4) * 2 + z}, device_id_type=MESH)
    pl.semaphore_signal(barrier, inc=1, device_id={"tp": y * 2 + 1 - z}, device_id_type=MESH)
    row = lax.broadcasted_iota(jnp.int32, (FINE, FINE), 0)
    col = lax.broadcasted_iota(jnp.int32, (FINE, FINE), 1)
    eye[...] = jnp.where(row == col, 1.0, 0.0).astype(bf16)
    for load in loads[:3]:
        load.wait()
    pl.semaphore_wait(barrier, SEQ + 3)

    def spread(part, block):
        @pl.loop(0, 8)
        def _(i):
            peer = block * 8 + (lax.rem(me, 8) ^ (7 - i))

            @pl.when(peer != me)
            def _():
                pltpu.make_async_remote_copy(
                    send.at[part, peer], recv.at[part, me], send_sem.at[part], recv_sem.at[part],
                    device_id={"seq": peer}, device_id_type=MESH,
                ).start()

    @pl.loop(0, 4)
    def _(step):
        block = lax.rem(me // 8 + 1 + step, 4)
        cols = pl.ds(pl.multiple_of(block * FINE, FINE), FINE)
        product = (inner[:, cols].astype(f32) * values[:, cols].astype(f32)).astype(bf16)
        for kind, piece in enumerate((product, filters[:, cols].astype(bf16))):
            flat = lax.dot_general(eye[...], piece, NT, preferred_element_type=f32).astype(bf16).reshape(8, 2, PART, FINE)
            for part in range(2):
                send[part, pl.ds(block * 8, 8), kind] = flat[:, part]
        spread(0, block)

    @pl.loop(0, 4)
    def _(step):
        spread(1, lax.rem(me // 8 + 1 + step, 4))

    for part in range(2):
        recv[part, me] = send[part, me]
    for load in loads[3:6]:
        load.wait()

    def give_back(half, part):
        @pl.loop(1, SEQ)
        def _(i):
            peer = me ^ (SEQ - i)
            pltpu.make_async_remote_copy(
                conv.at[half, part, peer], turned.at[half, part, me], csend_sem.at[half, part], crecv_sem.at[half, part],
                device_id={"seq": peer}, device_id_type=MESH,
            ).start()

        turned[half, part, me] = conv[half, part, me]

    def wait_bytes(ref, sem):
        pltpu.make_async_copy(ref.at[pl.ds(0, SEQ - 1)], ref.at[pl.ds(0, SEQ - 1)], sem).wait()

    @pl.loop(0, 2)
    def _(part):
        wait_bytes(recv.at[part], recv_sem.at[part])

        @pl.when(part == 1)
        def _():
            give_back(0, 0)

        transform(part, recv, forward, back, twiddle, spec, waves, conv)

    give_back(0, 1)
    give_back(1, 0)
    give_back(1, 1)
    for load in loads[6:]:
        load.wait()

    def mix(half):
        for part in range(2):
            wait_bytes(turned.at[half, part], crecv_sem.at[half, part])
        rows = slice(half * 128, half * 128 + 128)

        @pl.loop(0, 4)
        def _(block):
            cols = pl.ds(pl.multiple_of(block * FINE, FINE), FINE)
            both = [turned[half, part, pl.ds(block * 8, 8)].reshape(8, 1, PART, 128) for part in range(2)]
            piece = jnp.concatenate(both, axis=1).reshape(FINE, 128)
            here = lax.dot_general(eye[:128, :128], piece, NT, preferred_element_type=f32)
            product = inner[rows, cols].astype(f32) * values[rows, cols].astype(f32)
            mixed[rows, cols] = (outer[rows, cols].astype(f32) * (here + skip[:, cols] * product)).astype(bf16)

    def shares(chunk, d):
        return pltpu.make_async_remote_copy(
            psend.at[chunk, d], precv.at[chunk, d], psend_sem.at[chunk, d], precv_sem.at[chunk, d],
            device_id={"tp": lax.rem(y + d, 4) * 2 + z}, device_id_type=MESH,
        )

    def swap(chunk):
        return pltpu.make_async_remote_copy(
            zsend.at[chunk], zrecv.at[chunk], zsend_sem.at[chunk], zrecv_sem.at[chunk],
            device_id={"tp": y * 2 + 1 - z}, device_id_type=MESH,
        )

    def produce(chunk):
        rows = slice(chunk * 64, chunk * 64 + 64)
        for d in (2, 1, 3, 0):
            target = lax.rem(y + d, 4)

            @pl.loop(0, 2)
            def _(piece):
                cols = pl.ds(pl.multiple_of(target * 1024 + piece * 512, 512), 512)
                psend[chunk, d, :, pl.ds(pl.multiple_of(piece * 512, 512), 512)] = jnp.dot(
                    mixed[rows, :], w[:, cols], preferred_element_type=f32
                ).astype(bf16)

            if d:
                shares(chunk, d).start()

    def add_up(chunk):
        for d in range(1, 4):
            shares(chunk, d).wait_recv()

        def total(half):
            cols = pl.ds(pl.multiple_of(half * 512, 512), 512)
            acc = psend[chunk, 0, :, cols].astype(f32)
            for d in range(1, 4):
                acc += precv[chunk, d, :, cols].astype(f32)
            return acc

        zsend[chunk] = total(1 - z).astype(bf16)
        swap(chunk).start()
        kept[chunk] = total(z)

    def finish(chunk):
        swap(chunk).wait()
        out[chunk * 64 : chunk * 64 + 64, :] = (kept[chunk] + zrecv[chunk].astype(f32)).astype(bf16)
        for d in range(1, 4):
            shares(chunk, d).wait_send()

    mix(0)
    produce(0)
    produce(1)
    mix(1)
    produce(2)
    add_up(0)
    produce(3)
    add_up(1)
    add_up(2)
    finish(0)
    add_up(3)
    finish(1)
    finish(2)
    finish(3)
    for part in range(2):
        wait_bytes(send.at[part], send_sem.at[part])
        for half in range(2):
            wait_bytes(conv.at[half, part], csend_sem.at[half, part])


def local(inner_gate, values, outer_gate, filters, skip_gain, w_out):
    f32, bf16 = jnp.float32, jnp.bfloat16
    dma = pltpu.SemaphoreType.DMA
    return pl.pallas_call(
        kernel,
        out_shape=jax.ShapeDtypeStruct((FINE, 512), bf16),
        in_specs=[pl.BlockSpec(memory_space=pl.ANY)] * 9,
        out_specs=pl.BlockSpec(memory_space=pltpu.VMEM),
        scratch_shapes=[
            pltpu.VMEM((FINE, 1024), bf16),
            pltpu.VMEM((FINE, 1024), bf16),
            pltpu.VMEM((FINE, 1024), bf16),
            pltpu.VMEM((FINE, 1024), f32),
            pltpu.VMEM((1, 1024), f32),
            pltpu.VMEM((1024, 4096), bf16),
            pltpu.VMEM((2 * FINE, 2 * FINE), bf16),
            pltpu.VMEM((2 * FINE, 2 * FINE), bf16),
            pltpu.VMEM((BINS, 4, FINE), f32),
            pltpu.VMEM((2, SEQ, 2, PART, FINE), bf16),
            pltpu.VMEM((2, SEQ, 2, PART, FINE), bf16),
            pltpu.VMEM((BINS, 2, PART, 2 * FINE), bf16),
            pltpu.VMEM((BINS, PART, 2 * FINE), f32),
            pltpu.VMEM((2, 2, SEQ, PART, 128), bf16),
            pltpu.VMEM((2, 2, SEQ, PART, 128), bf16),
            pltpu.VMEM((FINE, 1024), bf16),
            pltpu.VMEM((FINE, FINE), bf16),
            pltpu.VMEM((4, 4, 64, 1024), bf16),
            pltpu.VMEM((4, 4, 64, 1024), bf16),
            pltpu.VMEM((4, 64, 512), f32),
            pltpu.VMEM((4, 64, 512), bf16),
            pltpu.VMEM((4, 64, 512), bf16),
            dma((9,)),
            dma((2,)),
            dma((2,)),
            dma((2, 2)),
            dma((2, 2)),
            dma((4, 4)),
            dma((4, 4)),
            dma((4,)),
            dma((4,)),
        ],
        compiler_params=pltpu.CompilerParams(collective_id=0, has_side_effects=True, vmem_limit_bytes=56 * 2**20),
        name="hyena",
    )(inner_gate, values, outer_gate, filters, skip_gain.reshape(1, -1), w_out, *tables())


def solution(mesh):
    in_specs = (P("seq", "tp"), P("seq", "tp"), P("seq", "tp"), P("seq", "tp"), P("tp"), P("tp", None))
    return jax.shard_map(local, mesh=mesh, in_specs=in_specs, out_specs=P("seq", "tp"), check_vma=False)
```

time: 104 us -> 81.2 us (0.78)
  Pallas kernels: 92.5 us -> 79.4 us
  local copies, waits for them, and re-layouts: 10.8 us -> 1.67 us
    pallas_call x3 -> x1, Pallas kernels: 92.5 us -> 79.4 us  [local(): pl.pallas_call(kernel, out_shape=jax.ShapeDtypeStruct((FINE, 512), bf16),...]
    unnamed x21 -> x1, local copies, waits for them, and re-layouts: 10.8 us -> 1.67 us
where the time goes in v2:
time: 81.2 us; the launch traced here: 81.1 us
  Pallas kernels  79.4 us (98%)
  local copies, waits for them, and re-layouts  1.67 us (2%)
    pallas_call x1, Pallas kernels, local(): pl.pallas_call(kernel, out_shape=jax.ShapeDtypeStruct((FINE, 512), bf16),...  79.4 us
    unnamed x1, local copies, waits for them, and re-layouts  1.67 us

profile of v2, /device:TPU:1, one launch (start us, length us, event | category | flops | bytes accessed | tf_op | source)
XLA Modules:
  0.0 81.1 jit_solution(9644142552814456501)
XLA Ops:
  0.0 79.4 %hyena.1 = bf16[256,512]{1,0:T(8,128)(2,1)} custom-call(bf16[256,1024]{1,0:T(8,128)(2,1)} %inner_hbm.1, bf16[256,1024]{1,0:T(8,128)(2,1)} %values_hbm.1, bf16[256,1024]{1,0:T(8,128)(2,1)} %outer_hbm.1, f32[256,1024]{1,0:T(8,128)} %filters_hbm.1, f32[1,1024]{1,0:T(1,128)} %bitcast.1, bf16[1024,4096]{1,0:T(8,128)(2,1)} %w_hbm.1, ...), custom_call_target="tpu_custom_call" | custom-call | tf_op jit(solution)/shard_map/hyena/pallas_call | solution.py:354
  79.4 1.7 %copy.11 = bf16[256,512]{1,0:T(8,128)(2,1)} copy(bf16[256,512]{1,0:T(8,128)(2,1)} %hyena.1) | data formatting | bytes 524288

commit v3 on v2

--- a/solution.py
+++ b/solution.py
@@ -15,6 +15,7 @@
 FINE = 256
 BINS = 33
 LENGTH = 2 * SEQ * FINE
+CHUNKS = ((0, 64), (64, 64), (128, 64), (192, 32), (224, 32))
 
 
 def twist(z, angle):
@@ -172,8 +173,8 @@
 def kernel(
     inner_hbm, values_hbm, outer_hbm, filters_hbm, skip_hbm, w_hbm, forward_hbm, back_hbm, twiddle_hbm, out,
     inner, values, outer, filters, skip, w, forward, back, twiddle,
-    send, recv, spec, waves, conv, turned, mixed, eye, psend, precv, kept, zsend, zrecv,
-    load_sem, send_sem, recv_sem, csend_sem, crecv_sem, psend_sem, precv_sem, zsend_sem, zrecv_sem,
+    send, recv, spec, waves, conv, turned, mixed, eye, psend, passed, precv, kept, zsend, zrecv,
+    load_sem, send_sem, recv_sem, csend_sem, crecv_sem, rsend_sem, rrecv_sem, psend_sem, precv_sem, zsend_sem, zrecv_sem,
 ):
     f32 = jnp.float32
     bf16 = jnp.bfloat16
@@ -194,7 +195,7 @@
     def _(i):
         pl.semaphore_signal(barrier, inc=1, device_id={"seq": me ^ i}, device_id_type=MESH)
 
-    for d in range(1, 4):
+    for d in (1, 3):
         pl.semaphore_signal(barrier, inc=1, device_id={"tp": lax.rem(y + d, 4) * 2 + z}, device_id_type=MESH)
     pl.semaphore_signal(barrier, inc=1, device_id={"tp": y * 2 + 1 - z}, device_id_type=MESH)
     row = lax.broadcasted_iota(jnp.int32, (FINE, FINE), 0)
@@ -202,7 +203,6 @@
     eye[...] = jnp.where(row == col, 1.0, 0.0).astype(bf16)
     for load in loads[:3]:
         load.wait()
-    pl.semaphore_wait(barrier, SEQ + 3)
 
     def spread(part, block):
         @pl.loop(0, 8)
@@ -216,15 +216,23 @@
                     device_id={"seq": peer}, device_id_type=MESH,
                 ).start()
 
-    @pl.loop(0, 4)
-    def _(step):
-        block = lax.rem(me // 8 + 1 + step, 4)
+    def pack(block):
         cols = pl.ds(pl.multiple_of(block * FINE, FINE), FINE)
         product = (inner[:, cols].astype(f32) * values[:, cols].astype(f32)).astype(bf16)
         for kind, piece in enumerate((product, filters[:, cols].astype(bf16))):
             flat = lax.dot_general(eye[...], piece, NT, preferred_element_type=f32).astype(bf16).reshape(8, 2, PART, FINE)
             for part in range(2):
                 send[part, pl.ds(block * 8, 8), kind] = flat[:, part]
+
+    first = lax.rem(me // 8 + 1, 4)
+    pack(first)
+    pl.semaphore_wait(barrier, SEQ + 2)
+    spread(0, first)
+
+    @pl.loop(1, 4)
+    def _(step):
+        block = lax.rem(me // 8 + 1 + step, 4)
+        pack(block)
         spread(0, block)
 
     @pl.loop(0, 4)
@@ -280,68 +288,104 @@
             product = inner[rows, cols].astype(f32) * values[rows, cols].astype(f32)
             mixed[rows, cols] = (outer[rows, cols].astype(f32) * (here + skip[:, cols] * product)).astype(bf16)
 
-    def shares(chunk, d):
+    def beside(step):
+        return {"tp": lax.rem(y + 1 + 2 * step, 4) * 2 + z}
+
+    def relay(chunk, step):
+        rows = pl.ds(0, CHUNKS[chunk][1])
         return pltpu.make_async_remote_copy(
-            psend.at[chunk, d], precv.at[chunk, d], psend_sem.at[chunk, d], precv_sem.at[chunk, d],
-            device_id={"tp": lax.rem(y + d, 4) * 2 + z}, device_id_type=MESH,
+            psend.at[chunk, 2, step, rows], passed.at[chunk, step, rows], rsend_sem.at[chunk, step], rrecv_sem.at[chunk, step],
+            device_id=beside(step), device_id_type=MESH,
         )
 
+    def share(chunk, step, piece):
+        rows = pl.ds(0, CHUNKS[chunk][1])
+        return pltpu.make_async_remote_copy(
+            psend.at[chunk, 1 + 2 * step, piece, rows], precv.at[chunk, step, piece, rows],
+            psend_sem.at[chunk, step, piece], precv_sem.at[chunk, step, piece],
+            device_id=beside(step), device_id_type=MESH,
+        )
+
     def swap(chunk):
+        rows = pl.ds(0, CHUNKS[chunk][1])
         return pltpu.make_async_remote_copy(
-            zsend.at[chunk], zrecv.at[chunk], zsend_sem.at[chunk], zrecv_sem.at[chunk],
+            zsend.at[chunk, rows], zrecv.at[chunk, rows], zsend_sem.at[chunk], zrecv_sem.at[chunk],
             device_id={"tp": y * 2 + 1 - z}, device_id_type=MESH,
         )
 
     def produce(chunk):
-        rows = slice(chunk * 64, chunk * 64 + 64)
+        start, count = CHUNKS[chunk]
         for d in (2, 1, 3, 0):
             target = lax.rem(y + d, 4)
 
             @pl.loop(0, 2)
             def _(piece):
                 cols = pl.ds(pl.multiple_of(target * 1024 + piece * 512, 512), 512)
-                psend[chunk, d, :, pl.ds(pl.multiple_of(piece * 512, 512), 512)] = jnp.dot(
-                    mixed[rows, :], w[:, cols], preferred_element_type=f32
+                psend[chunk, d, piece, 0:count] = jnp.dot(
+                    mixed[start : start + count, :], w[:, cols], preferred_element_type=f32
                 ).astype(bf16)
 
-            if d:
-                shares(chunk, d).start()
+            if d == 2:
+                relay(chunk, 0).start()
+                relay(chunk, 1).start()
+            elif d:
+                share(chunk, d // 2, 1 - d // 2).start()
+
+    def forward_on(chunk):
+        count = CHUNKS[chunk][1]
+        for step in range(2):
+            relay(chunk, step).wait_recv()
+            both = psend[chunk, 1 + 2 * step, step, 0:count].astype(f32) + passed[chunk, step, 0:count].astype(f32)
+            psend[chunk, 1 + 2 * step, step, 0:count] = both.astype(bf16)
+            share(chunk, step, step).start()
 
     def add_up(chunk):
-        for d in range(1, 4):
-            shares(chunk, d).wait_recv()
-
-        def total(half):
-            cols = pl.ds(pl.multiple_of(half * 512, 512), 512)
-            acc = psend[chunk, 0, :, cols].astype(f32)
-            for d in range(1, 4):
-                acc += precv[chunk, d, :, cols].astype(f32)
+        count = CHUNKS[chunk][1]
+        for step in range(2):
+            for piece in range(2):
+                share(chunk, step, piece).wait_recv()
+
+        def total(piece):
+            acc = psend[chunk, 0, piece, 0:count].astype(f32)
+            for step in range(2):
+                acc += precv[chunk, step, piece, 0:count].astype(f32)
             return acc
 
-        zsend[chunk] = total(1 - z).astype(bf16)
+        zsend[chunk, 0:count] = total(1 - z).astype(bf16)
         swap(chunk).start()
-        kept[chunk] = total(z)
+        kept[chunk, 0:count] = total(z)
 
     def finish(chunk):
+        start, count = CHUNKS[chunk]
         swap(chunk).wait()
-        out[chunk * 64 : chunk * 64 + 64, :] = (kept[chunk] + zrecv[chunk].astype(f32)).astype(bf16)
-        for d in range(1, 4):
-            shares(chunk, d).wait_send()
+        out[start : start + count, :] = (kept[chunk, 0:count] + zrecv[chunk, 0:count].astype(f32)).astype(bf16)
 
     mix(0)
     produce(0)
     produce(1)
+    forward_on(0)
+    forward_on(1)
     mix(1)
     produce(2)
     add_up(0)
     produce(3)
+    forward_on(2)
     add_up(1)
+    produce(4)
+    forward_on(3)
     add_up(2)
+    forward_on(4)
     finish(0)
     add_up(3)
     finish(1)
-    finish(2)
-    finish(3)
+    add_up(4)
+    for chunk in range(2, 5):
+        finish(chunk)
+    for chunk in range(5):
+        for step in range(2):
+            relay(chunk, step).wait_send()
+            for piece in range(2):
+                share(chunk, step, piece).wait_send()
     for part in range(2):
         wait_bytes(send.at[part], send_sem.at[part])
         for half in range(2):
@@ -374,20 +418,23 @@
             pltpu.VMEM((2, 2, SEQ, PART, 128), bf16),
             pltpu.VMEM((FINE, 1024), bf16),
             pltpu.VMEM((FINE, FINE), bf16),
-            pltpu.VMEM((4, 4, 64, 1024), bf16),
-            pltpu.VMEM((4, 4, 64, 1024), bf16),
-            pltpu.VMEM((4, 64, 512), f32),
-            pltpu.VMEM((4, 64, 512), bf16),
-            pltpu.VMEM((4, 64, 512), bf16),
+            pltpu.VMEM((5, 4, 2, 64, 512), bf16),
+            pltpu.VMEM((5, 2, 64, 512), bf16),
+            pltpu.VMEM((5, 2, 2, 64, 512), bf16),
+            pltpu.VMEM((5, 64, 512), f32),
+            pltpu.VMEM((5, 64, 512), bf16),
+            pltpu.VMEM((5, 64, 512), bf16),
             dma((9,)),
             dma((2,)),
             dma((2,)),
             dma((2, 2)),
             dma((2, 2)),
-            dma((4, 4)),
-            dma((4, 4)),
-            dma((4,)),
-            dma((4,)),
+            dma((5, 2)),
+            dma((5, 2)),
+            dma((5, 2, 2)),
+            dma((5, 2, 2)),
+            dma((5,)),
+            dma((5,)),
         ],
         compiler_params=pltpu.CompilerParams(collective_id=0, has_side_effects=True, vmem_limit_bytes=56 * 2**20),
         name="hyena",

time: 81.2 us -> 73.8 us (0.909)
  Pallas kernels: 79.4 us -> 72 us
    pallas_call x1, Pallas kernels: 79.4 us -> 72 us  [local(): pl.pallas_call(kernel, out_shape=jax.ShapeDtypeStruct((FINE, 512), bf16),...]
where the time goes in v3:
time: 73.8 us; the launch traced here: 73.7 us
  Pallas kernels  72 us (98%)
  local copies, waits for them, and re-layouts  1.67 us (2%)
    pallas_call x1, Pallas kernels, local(): pl.pallas_call(kernel, out_shape=jax.ShapeDtypeStruct((FINE, 512), bf16),...  72 us
    unnamed x1, local copies, waits for them, and re-layouts  1.67 us

profile of v3, /device:TPU:1, one launch (start us, length us, event | category | flops | bytes accessed | tf_op | source)
XLA Modules:
  0.0 73.7 jit_solution(11748859622684318601)
XLA Ops:
  0.0 72.0 %hyena.1 = bf16[256,512]{1,0:T(8,128)(2,1)} custom-call(bf16[256,1024]{1,0:T(8,128)(2,1)} %inner_hbm.1, bf16[256,1024]{1,0:T(8,128)(2,1)} %values_hbm.1, bf16[256,1024]{1,0:T(8,128)(2,1)} %outer_hbm.1, f32[256,1024]{1,0:T(8,128)} %filters_hbm.1, f32[1,1024]{1,0:T(1,128)} %bitcast.1, bf16[1024,4096]{1,0:T(8,128)(2,1)} %w_hbm.1, ...), custom_call_target="tpu_custom_call" | custom-call | tf_op jit(solution)/shard_map/hyena/pallas_call | solution.py:398
  72.0 1.7 %copy.11 = bf16[256,512]{1,0:T(8,128)(2,1)} copy(bf16[256,512]{1,0:T(8,128)(2,1)} %hyena.1) | data formatting | bytes 524288

commit v4 on v3

--- a/solution.py
+++ b/solution.py
@@ -15,7 +15,7 @@
 FINE = 256
 BINS = 33
 LENGTH = 2 * SEQ * FINE
-CHUNKS = ((0, 64), (64, 64), (128, 64), (192, 32), (224, 32))
+CHUNKS = ((0, 64), (64, 64), (128, 64), (192, 64))
 
 
 def twist(z, angle):
@@ -144,7 +144,7 @@
                 spec[k, kind, :, lanes] = a.astype(bf16)
                 spec[k, kind, :, lane * 128 + FINE : lane * 128 + FINE + 128] = b.astype(bf16)
 
-    group = 11
+    group = 33
 
     @pl.loop(0, BINS // group)
     def _(step):
@@ -313,23 +313,27 @@
             device_id={"tp": y * 2 + 1 - z}, device_id_type=MESH,
         )
 
-    def produce(chunk):
-        start, count = CHUNKS[chunk]
+    def produce(half):
+        chunks = [c for c, (start, _) in enumerate(CHUNKS) if start // 128 == half]
         for d in (2, 1, 3, 0):
             target = lax.rem(y + d, 4)
 
             @pl.loop(0, 2)
             def _(piece):
                 cols = pl.ds(pl.multiple_of(target * 1024 + piece * 512, 512), 512)
-                psend[chunk, d, piece, 0:count] = jnp.dot(
-                    mixed[start : start + count, :], w[:, cols], preferred_element_type=f32
+                part = jnp.dot(
+                    mixed[half * 128 : half * 128 + 128, :], w[:, cols], preferred_element_type=f32
                 ).astype(bf16)
-
-            if d == 2:
-                relay(chunk, 0).start()
-                relay(chunk, 1).start()
-            elif d:
-                share(chunk, d // 2, 1 - d // 2).start()
+                for c in chunks:
+                    start, count = CHUNKS[c]
+                    psend[c, d, piece, 0:count] = part[start - half * 128 : start - half * 128 + count]
+
+            for c in chunks:
+                if d == 2:
+                    relay(c, 0).start()
+                    relay(c, 1).start()
+                elif d:
+                    share(c, d // 2, 1 - d // 2).start()
 
     def forward_on(chunk):
         count = CHUNKS[chunk][1]
@@ -362,26 +366,21 @@
 
     mix(0)
     produce(0)
-    produce(1)
     forward_on(0)
     forward_on(1)
     mix(1)
-    produce(2)
+    produce(1)
     add_up(0)
-    produce(3)
+    add_up(1)
     forward_on(2)
-    add_up(1)
-    produce(4)
     forward_on(3)
+    finish(0)
     add_up(2)
-    forward_on(4)
-    finish(0)
+    finish(1)
     add_up(3)
-    finish(1)
-    add_up(4)
-    for chunk in range(2, 5):
-        finish(chunk)
-    for chunk in range(5):
+    finish(2)
+    finish(3)
+    for chunk in range(len(CHUNKS)):
         for step in range(2):
             relay(chunk, step).wait_send()
             for piece in range(2):
@@ -418,23 +417,23 @@
             pltpu.VMEM((2, 2, SEQ, PART, 128), bf16),
             pltpu.VMEM((FINE, 1024), bf16),
             pltpu.VMEM((FINE, FINE), bf16),
-            pltpu.VMEM((5, 4, 2, 64, 512), bf16),
-            pltpu.VMEM((5, 2, 64, 512), bf16),
-            pltpu.VMEM((5, 2, 2, 64, 512), bf16),
-            pltpu.VMEM((5, 64, 512), f32),
-            pltpu.VMEM((5, 64, 512), bf16),
-            pltpu.VMEM((5, 64, 512), bf16),
+            pltpu.VMEM((4, 4, 2, 64, 512), bf16),
+            pltpu.VMEM((4, 2, 64, 512), bf16),
+            pltpu.VMEM((4, 2, 2, 64, 512), bf16),
+            pltpu.VMEM((4, 64, 512), f32),
+            pltpu.VMEM((4, 64, 512), bf16),
+            pltpu.VMEM((4, 64, 512), bf16),
             dma((9,)),
             dma((2,)),
             dma((2,)),
             dma((2, 2)),
             dma((2, 2)),
-            dma((5, 2)),
-            dma((5, 2)),
-            dma((5, 2, 2)),
-            dma((5, 2, 2)),
-            dma((5,)),
-            dma((5,)),
+            dma((4, 2)),
+            dma((4, 2)),
+            dma((4, 2, 2)),
+            dma((4, 2, 2)),
+            dma((4,)),
+            dma((4,)),
         ],
         compiler_params=pltpu.CompilerParams(collective_id=0, has_side_effects=True, vmem_limit_bytes=56 * 2**20),
         name="hyena",

time: 73.8 us -> 72.9 us (0.988); the launches traced: 73.7 us -> 71.5 us
  Pallas kernels: 72 us -> 69.8 us
    pallas_call x1, Pallas kernels: 72 us -> 69.8 us  [local(): pl.pallas_call(kernel, out_shape=jax.ShapeDtypeStruct((FINE, 512), bf16),...]
where the time goes in v4:
time: 72.9 us; the launch traced here: 71.5 us
  Pallas kernels  69.8 us (96%)
  local copies, waits for them, and re-layouts  1.67 us (2%)
    pallas_call x1, Pallas kernels, local(): pl.pallas_call(kernel, out_shape=jax.ShapeDtypeStruct((FINE, 512), bf16),...  69.8 us
    unnamed x1, local copies, waits for them, and re-layouts  1.67 us

profile of v4, /device:TPU:1, one launch (start us, length us, event | category | flops | bytes accessed | tf_op | source)
XLA Modules:
  0.0 71.5 jit_solution(10575683647797608990)
XLA Ops:
  0.0 69.8 %hyena.1 = bf16[256,512]{1,0:T(8,128)(2,1)} custom-call(bf16[256,1024]{1,0:T(8,128)(2,1)} %inner_hbm.1, bf16[256,1024]{1,0:T(8,128)(2,1)} %values_hbm.1, bf16[256,1024]{1,0:T(8,128)(2,1)} %outer_hbm.1, f32[256,1024]{1,0:T(8,128)} %filters_hbm.1, f32[1,1024]{1,0:T(1,128)} %bitcast.1, bf16[1024,4096]{1,0:T(8,128)(2,1)} %w_hbm.1, ...), custom_call_target="tpu_custom_call" | custom-call | tf_op jit(solution)/shard_map/hyena/pallas_call | solution.py:397
  69.8 1.7 %copy.11 = bf16[256,512]{1,0:T(8,128)(2,1)} copy(bf16[256,512]{1,0:T(8,128)(2,1)} %hyena.1) | data formatting | bytes 524288

commit v5 on v4

--- a/solution.py
+++ b/solution.py
@@ -118,11 +118,13 @@
     return (
         jnp.asarray(forward, jnp.bfloat16),
         jnp.asarray(back, jnp.bfloat16),
-        jnp.asarray(twiddle, jnp.float32),
+        jnp.asarray(np.pad(twiddle, ((0, 2 * BINS), (0, 4), (0, 0))), jnp.float32),
     )
 
 
 def identity():
+    for load in loads:
+        load.start()
     row = lax.broadcasted_iota(jnp.int32, (FINE, FINE), 0)
     col = lax.broadcasted_iota(jnp.int32, (FINE, FINE), 1)
     return jnp.where(row == col, 1.0, 0.0).astype(jnp.bfloat16)
@@ -184,11 +186,9 @@
         pltpu.make_async_copy(a, b, load_sem.at[i])
         for i, (a, b) in enumerate((
             (inner_hbm, inner), (values_hbm, values), (filters_hbm, filters), (forward_hbm, forward), (back_hbm, back),
-            (twiddle_hbm, twiddle), (outer_hbm, outer), (skip_hbm, skip), (w_hbm, w),
+            (twiddle_hbm.at[pl.ds(0, BINS)], twiddle), (outer_hbm, outer), (skip_hbm, skip), (w_hbm, w),
         ))
     ]
-    for load in loads:
-        load.start()
     barrier = pltpu.get_barrier_semaphore()
 
     @pl.loop(1, SEQ)
@@ -198,6 +198,8 @@
     for d in (1, 3):
         pl.semaphore_signal(barrier, inc=1, device_id={"tp": lax.rem(y + d, 4) * 2 + z}, device_id_type=MESH)
     pl.semaphore_signal(barrier, inc=1, device_id={"tp": y * 2 + 1 - z}, device_id_type=MESH)
+    for load in loads:
+        load.start()
     row = lax.broadcasted_iota(jnp.int32, (FINE, FINE), 0)
     col = lax.broadcasted_iota(jnp.int32, (FINE, FINE), 1)
     eye[...] = jnp.where(row == col, 1.0, 0.0).astype(bf16)
@@ -408,7 +410,7 @@
             pltpu.VMEM((1024, 4096), bf16),
             pltpu.VMEM((2 * FINE, 2 * FINE), bf16),
             pltpu.VMEM((2 * FINE, 2 * FINE), bf16),
-            pltpu.VMEM((BINS, 4, FINE), f32),
+            pltpu.VMEM((BINS, 8, FINE), f32),
             pltpu.VMEM((2, SEQ, 2, PART, FINE), bf16),
             pltpu.VMEM((2, SEQ, 2, PART, FINE), bf16),
             pltpu.VMEM((BINS, 2, PART, 2 * FINE), bf16),
@@ -435,7 +437,7 @@
             dma((4,)),
             dma((4,)),
         ],
-        compiler_params=pltpu.CompilerParams(collective_id=0, has_side_effects=True, vmem_limit_bytes=56 * 2**20),
+        compiler_params=pltpu.CompilerParams(collective_id=0, has_side_effects=True, vmem_limit_bytes=56098816),
         name="hyena",
     )(inner_gate, values, outer_gate, filters, skip_gain.reshape(1, -1), w_out, *tables())
 

time: 72.9 us -> 71.7 us (0.984)
  Pallas kernels: 69.8 us -> 68.9 us
    pallas_call x1, Pallas kernels: 69.8 us -> 68.9 us  [local(): pl.pallas_call(kernel, out_shape=jax.ShapeDtypeStruct((FINE, 512), bf16),...]
    unnamed x1 -> x3, local copies, waits for them, and re-layouts: 1.67 us -> 1.39 us
where the time goes in v5:
time: 71.7 us; the launch traced here: 70.4 us
  Pallas kernels  68.9 us (96%)
  local copies, waits for them, and re-layouts  1.39 us (2%)
    pallas_call x1, Pallas kernels, local(): pl.pallas_call(kernel, out_shape=jax.ShapeDtypeStruct((FINE, 512), bf16),...  68.9 us

profile of v5, /device:TPU:1, one launch (start us, length us, event | category | flops | bytes accessed | tf_op | source)
XLA Modules:
  0.0 70.4 jit_solution(17517436831192913683)
XLA Ops:
  0.0 0.0 copy-start
  0.0 0.7 copy-done
  0.7 68.9 %hyena.1 = bf16[256,512]{1,0:T(8,128)(2,1)S(1)} custom-call(bf16[256,1024]{1,0:T(8,128)(2,1)} %inner_hbm.1, bf16[256,1024]{1,0:T(8,128)(2,1)} %values_hbm.1, bf16[256,1024]{1,0:T(8,128)(2,1)} %outer_hbm.1, f32[256,1024]{1,0:T(8,128)} %filters_hbm.1, f32[1,1024]{1,0:T(1,128)S(1)} %bitcast.1, bf16[1024,4096]{1,0:T(8,128)(2,1)} %w_hbm.1, ...), custom_call_target="tpu_custom_call" | custom-call | tf_op jit(solution)/shard_map/hyena/pallas_call | solution.py:399
  69.6 0.7 %copy.11 = bf16[256,512]{1,0:T(8,128)(2,1)} copy(bf16[256,512]{1,0:T(8,128)(2,1)S(1)} %hyena.1) | data formatting | bytes 524288
Async XLA Ops:
  0.0 0.7 copy-start

commit v6 on v5

--- a/solution.py
+++ b/solution.py
@@ -373,13 +373,13 @@
     mix(1)
     produce(1)
     add_up(0)
+    forward_on(2)
     add_up(1)
-    forward_on(2)
     forward_on(3)
+    add_up(2)
+    add_up(3)
     finish(0)
-    add_up(2)
     finish(1)
-    add_up(3)
     finish(2)
     finish(3)
     for chunk in range(len(CHUNKS)):

time: 71.7 us -> 71.6 us (level)
  no operation moved by 1% of the time
where the time goes in v6:
time: 71.6 us; the launch traced here: 70.4 us
  Pallas kernels  69 us (96%)
  local copies, waits for them, and re-layouts  1.39 us (2%)
    pallas_call x1, Pallas kernels, local(): pl.pallas_call(kernel, out_shape=jax.ShapeDtypeStruct((FINE, 512), bf16),...  69 us

profile of v6, /device:TPU:1, one launch (start us, length us, event | category | flops | bytes accessed | tf_op | source)
XLA Modules:
  0.0 70.4 jit_solution(4936091877816898664)
XLA Ops:
  0.0 0.0 copy-start
  0.0 0.7 copy-done
  0.7 69.0 %hyena.1 = bf16[256,512]{1,0:T(8,128)(2,1)S(1)} custom-call(bf16[256,1024]{1,0:T(8,128)(2,1)} %inner_hbm.1, bf16[256,1024]{1,0:T(8,128)(2,1)} %values_hbm.1, bf16[256,1024]{1,0:T(8,128)(2,1)} %outer_hbm.1, f32[256,1024]{1,0:T(8,128)} %filters_hbm.1, f32[1,1024]{1,0:T(1,128)S(1)} %bitcast.1, bf16[1024,4096]{1,0:T(8,128)(2,1)} %w_hbm.1, ...), custom_call_target="tpu_custom_call" | custom-call | tf_op jit(solution)/shard_map/hyena/pallas_call | solution.py:399
  69.7 0.7 %copy.11 = bf16[256,512]{1,0:T(8,128)(2,1)} copy(bf16[256,512]{1,0:T(8,128)(2,1)S(1)} %hyena.1) | data formatting | bytes 524288
Async XLA Ops:
  0.0 0.7 copy-start
